TPU v7x, 128 devices: a whole 4x4x4 slice. The times are simulated.
128 devices in a mesh: gx: 16 (over z, x), gy: 8 (over y, core).
Axes of the slice: x: 4, y: 4, z: 4, core: 2. Of those that a mesh axis runs over, the one named last changes fastest.
Arguments:
- clm_block: int32 [1048576], P(('gx', 'gy')), may hold values from 0 to 127, as said below
- clm_cell: int32 [1048576], P(('gx', 'gy')), may hold values from 0 to 8191, as said below
- precip: float32 [1048576], P(('gx', 'gy')), may hold values from 0.05 to 2
- evap_demand: float32 [1048576], P(('gx', 'gy')), may hold values from 0.05 to 1
- root_share: float32 [10, 1048576], P(None, ('gx', 'gy')), may hold values from 0.05 to 1
- sat_before: float32 [10, 1048576], P(None, ('gx', 'gy')), may hold values from 0.2 to 1
- pressure: float32 [10, 512, 2048], P(None, 'gx', 'gy'), may hold values from -3 to 0.5
- conductivity: float32 [10, 512, 2048], P(None, 'gx', 'gy'), may hold values from 0.1 to 3
- porosity: float32 [10, 512, 2048], P(None, 'gx', 'gy'), may hold values from 0.25 to 0.5
- freeze_state: int32 [10, 512, 2048], P(None, 'gx', 'gy'), may hold values from 0 to 2
- land_mask: int32 [512, 2048], P('gx', 'gy'), may hold values 0 or 1
Outputs:
- new_pressure: float32 [10, 512, 2048], P(None, 'gx', 'gy')
- returned_sat: float32 [10, 1048576], P(None, ('gx', 'gy'))
Inputs may be any that keep to these rules, and one draw needn't show every extreme that they name: Grid blocks are 32 x 256 columns, numbered with the second horizontal dimension fastest. Within one device's entries clm_block never falls; one device's entries name at most 96 columns of one block, and exactly that many for some blocks. `clm_cell`: together with clm_block, every grid column is named exactly once.
All inputs are finite; a program needn't handle non-finite values. No bound on the sum of `land_mask` on one device may be relied on, other than what follows from the above.
Results may differ from a plain program's by a relative error of at most 0.0002.
Values sent between devices are 32-bit elements; how exact they have to be, the bound alone decides.
A program may use at most 64 MiB of HBM per device.

v0:
```python
import functools

import jax
import jax.numpy as jnp
from jax import lax
from jax.experimental import pallas as pl
from jax.experimental.pallas import tpu as pltpu
from jax.sharding import PartitionSpec as P

MESH = pl.DeviceIdType.MESH
F32, BF16, I32 = jnp.float32, jnp.bfloat16, jnp.int32

NZ = 10
CX = 32
CY = 256
GX = 16
GY = 8
DEVICES = GX * GY
COLUMNS = CX * CY
HALO = 8
ROWS = CX + 2 * HALO
LANES = CY + 128
OMEGA = 0.8
VMEM_LIMIT = 56 * 1024 * 1024

VMEM = pl.BlockSpec(memory_space=pltpu.VMEM)
SMEM = pl.BlockSpec(memory_space=pltpu.SMEM)


def iota(shape, dim):
    return lax.broadcasted_iota(I32, shape, dim)


def params(**extra):
    return pltpu.CompilerParams(vmem_limit_bytes=VMEM_LIMIT, **extra)


def owner_ends(block_ref, row):
    owners = iota((DEVICES, 128), 0)

    def count(j, total):
        piece = block_ref[:, pl.ds(pl.multiple_of(j * 128, 128), 128)]
        return total + jnp.where(piece <= owners, 1.0, 0.0)

    total = lax.fori_loop(0, COLUMNS // 128, count, jnp.zeros((DEVICES, 128), F32), unroll=4)
    row[...] = lax.dot_general(
        jnp.ones((8, 128), BF16), total.astype(BF16), (((1,), (1,)), ((), ())), preferred_element_type=F32
    ).astype(I32)


def column_fluxes(cell_ref, precip_ref, evap_ref, root_ref, sat_ref, payload):
    width = 512

    def chunk(j, carry):
        at = pl.ds(pl.multiple_of(j * width, width), width)
        sat = sat_ref[:, at]
        weights = root_ref[:, at] * sat * sat
        total = 0.25 + jnp.sum(weights, axis=0, keepdims=True)
        uptake = evap_ref[:, at] * weights / total
        top = sat[0:1]
        infiltration = precip_ref[:, at] * (1.0 - top * top * top)
        payload[0:NZ, at] = jnp.where(iota((NZ, width), 0) == 0, infiltration, 0.0) - uptake
        payload[NZ : NZ + 1, at] = cell_ref[:, at].astype(F32)
        return carry

    lax.fori_loop(0, COLUMNS // width, chunk, 0)
    payload[:, COLUMNS : COLUMNS + 256] = jnp.zeros((16, 256), F32)


def run_of(ends, owner):
    end = ends[0, owner]
    start = jnp.where(owner == 0, 0, ends[0, jnp.maximum(owner - 1, 0)])
    base = pl.multiple_of((start // 128) * 128, 128)
    return start, end, base, start - base


def prep_kernel(block_ref, cell_ref, precip_ref, evap_ref, root_ref, sat_ref, messages_ref, ends_ref, payload, ends, sem):
    owner_ends(block_ref, ends_ref)
    copy = pltpu.make_async_copy(ends_ref, ends, sem)
    copy.start()
    column_fluxes(cell_ref, precip_ref, evap_ref, root_ref, sat_ref, payload)
    copy.wait()
    lane = iota((16, 128), 1)
    row = iota((16, 128), 0)

    def one(owner, carry):
        start, end, base, shift = run_of(ends, owner)
        amount = jnp.where(shift == 0, 0, 128 - shift)
        first = pltpu.roll(payload[:, pl.ds(base, 128)], amount, 1)
        second = pltpu.roll(payload[:, pl.ds(pl.multiple_of(base + 128, 128), 128)], amount, 1)
        slab = jnp.where(lane < 128 - shift, first, second)
        messages_ref[owner] = jnp.where((row == NZ) & (lane >= end - start), -1.0, slab)
        return carry

    lax.fori_loop(0, DEVICES, one, 0, unroll=4)


def unroute_kernel(ends, answer_ref, out_ref, wide):
    lane = iota((16, 128), 1)

    def one(owner, carry):
        _, _, base, shift = run_of(ends, owner)
        slab = pltpu.roll(answer_ref[owner], shift, 1)
        here = pl.ds(base, 128)
        wide[:, here] = jnp.where(lane >= shift, slab, wide[:, here])
        wide[:, pl.ds(pl.multiple_of(base + 128, 128), 128)] = slab
        return carry

    lax.fori_loop(0, DEVICES, one, 0, unroll=4)
    out_ref[...] = wide[0:NZ, 0:COLUMNS]


def position():
    return lax.axis_index("gx"), lax.axis_index("gy")


def device_at(offset):
    gx, gy = position()
    flat = lax.rem(gx * GY + gy + offset, DEVICES)
    return flat // GY, lax.rem(flat, GY)


def neighbour(dx, dy):
    gx, gy = position()
    return lax.rem(gx + dx + GX, GX), lax.rem(gy + dy + GY, GY)


def greet_all():
    barrier = pltpu.get_barrier_semaphore()

    def greet(k, carry):
        pl.semaphore_signal(barrier, inc=1, device_id=device_at(k), device_id_type=MESH)
        return carry

    lax.fori_loop(1, DEVICES, greet, 0)
    pl.semaphore_wait(barrier, DEVICES - 1)


def send_all(source, target, rows, send_sem, recv_sem):
    gx, gy = position()
    me = gx * GY + gy

    def send(k, carry):
        to = device_at(k)
        pltpu.make_async_remote_copy(
            src_ref=source.at[to[0] * GY + to[1], pl.ds(0, rows)],
            dst_ref=target.at[me, pl.ds(0, rows)],
            send_sem=send_sem,
            recv_sem=recv_sem,
            device_id=to,
            device_id_type=MESH,
        ).start()
        return carry

    lax.fori_loop(1, DEVICES, send, 0)
    target[me] = source[me]


def wait_all(source, target, rows, send_sem, recv_sem):
    part = (pl.ds(0, DEVICES - 1), pl.ds(0, rows))
    pltpu.make_async_copy(source.at[part], target.at[part], recv_sem).wait()
    pltpu.make_async_copy(source.at[part], target.at[part], send_sem).wait()


SIDES = tuple((dx, dy) for dx in (-1, 0, 1) for dy in (-1, 0, 1) if (dx, dy) != (0, 0))


def halo_copies(block, strips, x_halo, y_halo, send_sem, recv_sem):
    copies = []
    for at, (dx, dy) in enumerate(SIDES):
        from_rows = {-1: pl.ds(0, HALO), 0: pl.ds(0, CX), 1: pl.ds(CX - HALO, HALO)}[dx]
        to_rows = {-1: pl.ds(ROWS - HALO, HALO), 0: pl.ds(HALO, CX), 1: pl.ds(0, HALO)}[dx]
        if dy == 0:
            source, target = block.at[:, :, from_rows, :], x_halo.at[0 if dx == 1 else 1]
        else:
            source = strips.at[0 if dy == -1 else 1, :, from_rows, :]
            target = y_halo.at[0 if dy == 1 else 1, :, to_rows, :]
        copies.append(
            pltpu.make_async_remote_copy(
                src_ref=source,
                dst_ref=target,
                send_sem=send_sem.at[at],
                recv_sem=recv_sem.at[at],
                device_id=neighbour(dx, dy),
                device_id_type=MESH,
            )
        )
    return copies


def first_exchange_kernel(messages, block, strips, incoming, x_halo, y_halo, sems, halo_send, halo_recv):
    greet_all()
    copies = halo_copies(block, strips, x_halo, y_halo, halo_send, halo_recv)
    send_all(messages, incoming, NZ + 1, sems.at[0], sems.at[1])
    for copy in copies:
        copy.start()
    wait_all(messages, incoming, NZ + 1, sems.at[0], sems.at[1])
    for copy in copies:
        copy.wait()


def halo_kernel(block, strips, x_halo, y_halo, halo_send, halo_recv):
    barrier = pltpu.get_barrier_semaphore()
    for dx, dy in SIDES:
        pl.semaphore_signal(barrier, inc=1, device_id=neighbour(dx, dy), device_id_type=MESH)
    pl.semaphore_wait(barrier, len(SIDES))
    copies = halo_copies(block, strips, x_halo, y_halo, halo_send, halo_recv)
    for copy in copies:
        copy.start()
    for copy in copies:
        copy.wait()


def reply_kernel(reply, answer, sems):
    greet_all()
    send_all(reply, answer, NZ, sems.at[0], sems.at[1])
    wait_all(reply, answer, NZ, sems.at[0], sems.at[1])


def pack_strips(block, at, strips):
    group = iota((CX, 128), 1) // HALO
    low = jnp.zeros((CX, 128), F32)
    high = jnp.zeros((CX, 128), F32)
    for k in range(NZ):
        low = jnp.where(group == k, pltpu.roll(block[at, k, :, 0:128], HALO * k, 1), low)
        high = jnp.where(group == k, pltpu.roll(block[at, k, :, CY - 128 : CY], HALO * (k + 1), 1), high)
    strips[0, at] = low
    strips[1, at] = high


def block_kernel(pressure_ref, conductivity_ref, porosity_ref, freeze_ref, block, strips):
    freeze = freeze_ref[...]
    factor = jnp.where(freeze == 0, 1.0, jnp.where(freeze == 1, 0.2, 0.02)).astype(F32)
    block[0] = conductivity_ref[...] * factor
    block[1] = porosity_ref[...]
    block[2] = pressure_ref[...]
    for at in range(3):
        pack_strips(block, at, strips)


def widen(block, at, x_halo, y_halo, wide):
    lane = iota((ROWS, 128), 1)
    for k in range(NZ):
        wide[k, HALO : HALO + CX, 0:CY] = block[at, k]
        wide[k, 0:HALO, 0:CY] = x_halo[0, at, k]
        wide[k, HALO + CX : ROWS, 0:CY] = x_halo[1, at, k]
        low = pltpu.roll(y_halo[0, at], 120 - HALO * k, 1)
        high = pltpu.roll(y_halo[1, at], (128 - HALO * k) % 128, 1)
        wide[k, :, CY:LANES] = jnp.where(lane < HALO, high, jnp.where(lane >= 128 - HALO, low, 0.0))


def compact(ref, group):
    lane = iota((16, 128), 1)
    first, second, third, fourth = (ref[group * 4 + i] for i in range(4))
    second = pltpu.roll(second, 96, 1)
    third = pltpu.roll(third, 64, 1)
    fourth = pltpu.roll(fourth, 32, 1)
    return (
        jnp.where(lane < 96, first, second),
        jnp.where(lane < 64, second, third),
        jnp.where(lane < 32, third, fourth),
    )


def places(tile):
    cell = tile[NZ : NZ + 1].astype(I32)
    return cell >> 8, cell & (CY - 1)


def hot(index, size):
    return jnp.where(iota((size, index.shape[1]), 0) == index, 1.0, 0.0).astype(BF16)


def scatter_kernel(incoming, mask_ref, block, strips, total):
    total[...] = jnp.zeros_like(total)

    def step(j, carry):
        tiles = compact(incoming, 2 * j) + compact(incoming, 2 * j + 1)
        high_parts, low_parts, right_parts = [], [], []
        for tile in tiles:
            at_x, at_y = places(tile)
            hot_x = hot(at_x, CX)
            high = tile.astype(BF16).astype(F32)
            low = tile - high
            for part, into in ((high, high_parts), (low, low_parts)):
                rows = []
                for k in range(NZ):
                    spread = jnp.broadcast_to(part[k : k + 1], (16, 128)).astype(BF16)
                    rows += [spread * hot_x[0:16], spread * hot_x[16:32]]
                into.append(jnp.concatenate(rows, axis=0))
            right_parts.append(hot(at_y, CY))
        left = jnp.concatenate(high_parts + low_parts, axis=1)
        right = jnp.concatenate(right_parts + right_parts, axis=1)
        total[...] += lax.dot_general(left, right, (((1,), (1,)), ((), ())), preferred_element_type=F32)
        return carry

    lax.fori_loop(0, DEVICES // 8, step, 0)
    mask = mask_ref[...].astype(F32)
    for k in range(NZ):
        block[0, k] = total[k * CX : (k + 1) * CX] * mask
    pack_strips(block, 0, strips)


def up(field, dim):
    return pltpu.roll(field, field.shape[dim] - 1, dim)


def down(field, dim):
    return pltpu.roll(field, 1, dim)


def dry_inverse(field):
    dryness = jnp.maximum(-field, 0.0)
    return dryness, lax.rsqrt(1.0 + dryness * dryness)


def joined(one, two):
    both = one + two
    return one * two / jnp.where(both > 0.0, both, 1.0)


def newton_kernel(
    block, x_halo, y_halo, source, source_x, source_y, incoming, pressure_out, reply,
    perm, porosity, p, src, stored, kr, hx, hy, hz, gx_, gy_, gz, scale, start, u, v,
):
    gx, gy = position()
    widen(block, 0, x_halo, y_halo, perm)
    widen(block, 1, x_halo, y_halo, porosity)
    widen(block, 2, x_halo, y_halo, p)
    widen(source, 0, source_x, source_y, src)
    zero = jnp.zeros((ROWS, LANES), F32)
    row, lane = iota((ROWS, LANES), 0), iota((ROWS, LANES), 1)
    outside = ((row < HALO) & (gx == 0)) | ((row >= HALO + CX) & (gx == GX - 1))
    outside = outside | ((lane >= CY + 64) & (gy == 0)) | ((lane >= CY) & (lane < CY + 64) & (gy == GY - 1))
    p[NZ] = zero
    kr[NZ] = zero
    gz[0] = zero
    gz[NZ] = zero
    for ref in (u, v):
        ref[0] = zero
        ref[NZ + 1] = zero

    def prepare(k, carry):
        perm[k] = jnp.where(outside, 0.0, perm[k])
        return carry

    lax.fori_loop(0, NZ, prepare, 0)

    def faces(k, carry):
        here = perm[k]
        hx[k] = joined(here, up(here, 0))
        hy[k] = joined(here, up(here, 1))
        stored[k] = dry_inverse(p[k])[1]
        return carry

    lax.fori_loop(0, NZ, faces, 0)

    def vertical_faces(k, carry):
        hz[k] = joined(perm[k], perm[k + 1])
        return carry

    lax.fori_loop(0, NZ - 1, vertical_faces, 0)

    def newton(step, carry):
        def relative(k, carry):
            inverse = dry_inverse(p[k])[1]
            kr[k] = inverse * inverse * inverse
            return carry

        lax.fori_loop(0, NZ, relative, 0)

        def linearize(k, flow_above, last):
            here, rel = p[k], kr[k]
            side_x = hx[k] * (rel + up(rel, 0))
            side_y = hy[k] * (rel + up(rel, 1))
            gx_[k] = side_x
            gy_[k] = side_y
            flow_x = side_x * (here - up(here, 0))
            flow_y = side_y * (here - up(here, 1))
            above = gz[k]
            if last:
                flow = perm[k] * rel
            else:
                below = hz[k] * (rel + kr[k + 1])
                gz[k + 1] = below
                flow = below * (here - p[k + 1] + 1.0)
            dryness, inverse = dry_inverse(here)
            residual = porosity[k] * (inverse - stored[k]) + (flow_x - down(flow_x, 0)) + (flow_y - down(flow_y, 1))
            residual = residual + flow - flow_above - src[k]
            diagonal = porosity[k] * (dryness * rel) + side_x + down(side_x, 0) + side_y + down(side_y, 1) + above
            if not last:
                diagonal = diagonal + below
            diagonal = jnp.where(diagonal > 0.0, diagonal, 1.0)
            factor = OMEGA / diagonal
            scale[k] = factor
            first = -residual * factor
            start[k] = first
            u[k + 1] = first
            return flow

        flow = lax.fori_loop(0, NZ - 1, lambda k, f: linearize(k, f, False), zero)
        linearize(NZ - 1, flow, True)
        for old, new in ((u, v), (v, u), (u, v)):

            def sweep(k, carry, old=old, new=new):
                here = old[k + 1]
                side_x, side_y = gx_[k], gy_[k]
                coupled = side_x * up(here, 0) + down(side_x * here, 0) + side_y * up(here, 1) + down(side_y * here, 1)
                coupled = coupled + gz[k] * old[k] + gz[k + 1] * old[k + 2]
                new[k + 1] = (1.0 - OMEGA) * here + start[k] + scale[k] * coupled
                return carry

            lax.fori_loop(0, NZ, sweep, 0)

        def advance(k, carry):
            p[k] = p[k] + v[k + 1]
            return carry

        lax.fori_loop(0, NZ, advance, 0)
        return carry

    lax.fori_loop(0, 2, newton, 0)
    parts = []
    for k in range(NZ):
        final = p[k, HALO : HALO + CX, 0:CY]
        pressure_out[k] = final
        parts.append(dry_inverse(final)[1])
    saturated = jnp.concatenate(parts, axis=0)
    high = saturated.astype(BF16)
    left = jnp.concatenate([high, (saturated - high.astype(F32)).astype(BF16)], axis=1)
    gather(left, incoming, reply)


def gather(left, incoming, reply):
    lane = iota((16, 128), 1)

    def step(group, carry):
        outs = []
        for tile in compact(incoming, group):
            at_x, at_y = places(tile)
            hot_y = hot(at_y, CY)
            both = jnp.concatenate([hot_y, hot_y], axis=0)
            lines = jnp.dot(left, both, preferred_element_type=F32)
            here = iota((CX, 128), 0) == at_x
            rows = [
                jnp.sum(jnp.where(here, lines[k * CX : (k + 1) * CX], 0.0), axis=0, keepdims=True) for k in range(NZ)
            ]
            outs.append(jnp.concatenate(rows + [jnp.zeros((16 - NZ, 128), F32)], axis=0))
        one, two, three = outs
        reply[group * 4] = one
        reply[group * 4 + 1] = pltpu.roll(jnp.where(lane >= 96, one, two), 32, 1)
        reply[group * 4 + 2] = pltpu.roll(jnp.where(lane >= 64, two, three), 64, 1)
        reply[group * 4 + 3] = pltpu.roll(three, 96, 1)
        return carry

    lax.fori_loop(0, DEVICES // 4, step, 0)


def shaped(*lengths):
    return jax.ShapeDtypeStruct(lengths, F32)


def call(kernel, outs, scratch, extra=None, ins=None, count=None):
    return pl.pallas_call(
        kernel,
        out_shape=outs,
        in_specs=ins or [VMEM] * count,
        out_specs=jax.tree.map(lambda _: VMEM, outs),
        scratch_shapes=scratch,
        compiler_params=params(**(extra or {})),
    )


def on_device(
    clm_block, clm_cell, precip, evap_demand, root_share, sat_before,
    pressure, conductivity, porosity, freeze_state, land_mask,
):
    flat = [a.reshape(1, COLUMNS) for a in (clm_block, clm_cell, precip, evap_demand)]
    slabs = shaped(DEVICES, 16, 128)
    dma = pltpu.SemaphoreType.DMA
    messages, ends = call(
        prep_kernel,
        (slabs, jax.ShapeDtypeStruct((8, 128), I32)),
        [pltpu.VMEM((16, COLUMNS + 256), F32), pltpu.SMEM((8, 128), I32), dma],
        count=6,
    )(*flat, root_share, sat_before)
    block, strips = call(block_kernel, (shaped(3, NZ, CX, CY), shaped(2, 3, CX, 128)), [], count=4)(
        pressure, conductivity, porosity, freeze_state
    )
    incoming, x_halo, y_halo = call(
        first_exchange_kernel,
        (slabs, shaped(2, 3, NZ, HALO, CY), shaped(2, 3, ROWS, 128)),
        [dma((2,)), dma((8,)), dma((8,))],
        dict(collective_id=0, has_side_effects=True),
        count=3,
    )(messages, block, strips)
    source, source_strips = call(
        scatter_kernel, (shaped(1, NZ, CX, CY), shaped(2, 1, CX, 128)), [pltpu.VMEM((NZ * CX, CY), F32)], count=2
    )(incoming, land_mask)
    source_x, source_y = call(
        halo_kernel,
        (shaped(2, 1, NZ, HALO, CY), shaped(2, 1, ROWS, 128)),
        [dma((8,)), dma((8,))],
        dict(collective_id=1, has_side_effects=True),
        count=2,
    )(source, source_strips)
    wide = lambda n: pltpu.VMEM((n, ROWS, LANES), F32)
    counts = (NZ, NZ, NZ + 1, NZ, NZ, NZ + 1, NZ, NZ, NZ, NZ, NZ, NZ + 1, NZ, NZ, NZ + 2, NZ + 2)
    new_pressure, reply = call(
        newton_kernel, (shaped(NZ, CX, CY), slabs), [wide(n) for n in counts], count=7
    )(block, x_halo, y_halo, source, source_x, source_y, incoming)
    answer = call(
        reply_kernel, slabs, [dma((2,))], dict(collective_id=2, has_side_effects=True), count=1
    )(reply)
    returned = call(
        unroute_kernel, shaped(NZ, COLUMNS), [pltpu.VMEM((16, COLUMNS + 256), F32)], ins=[SMEM, VMEM]
    )(ends, answer)
    return new_pressure, returned


def solution(mesh):
    both = P(("gx", "gy"))
    columns = P(None, ("gx", "gy"))
    grid = P(None, "gx", "gy")
    return jax.shard_map(
        on_device,
        mesh=mesh,
        in_specs=(both, both, both, both, columns, columns, grid, grid, grid, grid, P("gx", "gy")),
        out_specs=(grid, columns),
        check_vma=False,
    )
```

profile of v0, /device:TPU:1, one launch (start us, length us, event | category | flops | bytes accessed | tf_op | source)
XLA Modules:
  0.0 125.1 jit_solution(3400130827413409696)
XLA Ops:
  0.6 7.1 %shard_map.123 = (f32[128,16,128]{2,1,0:T(8,128)}, s32[8,128]{1,0:T(8,128)}) custom-call(s32[1,8192]{1,0:T(1,128)} %bitcast.4, s32[1,8192]{1,0:T(1,128)} %bitcast.5, f32[1,8192]{1,0:T(1,128)} %bitcast.6, f32[1,8192]{1,0:T(1,128)} %bitcast.7, f32[10,8192]{1,0:T(8,128)} %root_ref.1, f32[10,8192]{1,0:T(8,128)} %sat_ref.1), custom_call_target="tpu_custom_call" | custom-call | tf_op jit(solution)/shard_map/pallas_call | solution.py:481
  7.7 2.4 %shard_map.122 = (f32[3,10,32,256]{3,2,1,0:T(8,128)}, f32[2,3,32,128]{3,2,1,0:T(8,128)}) custom-call(f32[10,32,256]{2,1,0:T(8,128)} %pressure_ref.1, f32[10,32,256]{2,1,0:T(8,128)} %conductivity_ref.1, f32[10,32,256]{2,1,0:T(8,128)} %porosity_ref.1, s32[10,32,256]{2,1,0:T(8,128)} %freeze_ref.1), custom_call_target="tpu_custom_call" | custom-call | tf_op jit(solution)/shard_map/pallas_call | solution.py:487
  10.1 31.4 %shard_map.124 = (f32[128,16,128]{2,1,0:T(8,128)}, f32[2,3,10,8,256]{4,3,2,1,0:T(8,128)}, f32[2,3,48,128]{3,2,1,0:T(8,128)}) custom-call(f32[128,16,128]{2,1,0:T(8,128)} %get-tuple-element.16.messages, f32[3,10,32,256]{3,2,1,0:T(8,128)} %get-tuple-element.15.block, f32[2,3,32,128]{3,2,1,0:T(8,128)} %get-tuple-element.17.strips), custom_call_target="tpu_custom_call" | custom-call | tf_op jit(solution)/shard_map/pallas_call | solution.py:490
  41.6 10.7 %shard_map.125 = (f32[1,10,32,256]{3,2,1,0:T(8,128)}, f32[2,1,32,128]{3,2,1,0:T(8,128)}) custom-call(f32[128,16,128]{2,1,0:T(8,128)} %get-tuple-element.20.incoming, s32[32,256]{1,0:T(8,128)} %mask_ref.1), custom_call_target="tpu_custom_call" | custom-call | tf_op jit(solution)/shard_map/pallas_call | solution.py:497
  52.3 10.8 %shard_map.126 = (f32[2,1,10,8,256]{4,3,2,1,0:T(8,128)}, f32[2,1,48,128]{3,2,1,0:T(8,128)}) custom-call(f32[1,10,32,256]{3,2,1,0:T(8,128)} %get-tuple-element.21.block.source, f32[2,1,32,128]{3,2,1,0:T(8,128)} %get-tuple-element.22.strips), custom_call_target="tpu_custom_call" | custom-call | tf_op jit(solution)/shard_map/pallas_call | solution.py:500
  63.1 36.2 %shard_map.127 = (f32[10,32,256]{2,1,0:T(8,128)}, f32[128,16,128]{2,1,0:T(8,128)}) custom-call(f32[3,10,32,256]{3,2,1,0:T(8,128)} %get-tuple-element.15.block, f32[2,3,10,8,256]{4,3,2,1,0:T(8,128)} %get-tuple-element.18.x_halo, f32[2,3,48,128]{3,2,1,0:T(8,128)} %get-tuple-element.19.y_halo, f32[1,10,32,256]{3,2,1,0:T(8,128)} %get-tuple-element.21.block.source, ...), custom_call_target="tpu_custom_call" | custom-call | tf_op jit(solution)/shard_map/pallas_call | solution.py:509
  99.3 20.8 %shard_map.128.answer_ref = f32[128,16,128]{2,1,0:T(8,128)} custom-call(f32[128,16,128]{2,1,0:T(8,128)} %get-tuple-element.27.reply), custom_call_target="tpu_custom_call" | custom-call | tf_op jit(solution)/shard_map/pallas_call | solution.py:512
  120.1 5.1 %shard_map.129 = f32[10,8192]{1,0:T(8,128)} custom-call(s32[8,128]{1,0:T(8,128)} %get-tuple-element.26.ends, f32[128,16,128]{2,1,0:T(8,128)} %shard_map.128.answer_ref), custom_call_target="tpu_custom_call" | custom-call | tf_op jit(solution)/shard_map/pallas_call | solution.py:515
where the time goes:
time: 125 us
  Pallas kernels  124 us (99%)
    pallas_call x1, Pallas kernels, on_device(): call(newton_kernel, (shaped(NZ, CX, CY), slabs), [wide(n) for n in counts...  36.2 us
    pallas_call x1, Pallas kernels, on_device(): call(first_exchange_kernel, (slabs, shaped(2, 3, NZ, HALO, CY), shaped(2,...  31.4 us
    pallas_call x1, Pallas kernels, on_device(): call(reply_kernel, slabs, [dma((2,))], dict(collective_id=2, has_side_eff...  20.8 us
    pallas_call x1, Pallas kernels, on_device(): call(halo_kernel, (shaped(2, 1, NZ, HALO, CY), shaped(2, 1, ROWS, 128)),...  10.8 us
    pallas_call x1, Pallas kernels, on_device(): call(scatter_kernel, (shaped(1, NZ, CX, CY), shaped(2, 1, CX, 128)), [plt...  10.7 us
    pallas_call x1, Pallas kernels, on_device(): call(prep_kernel, (slabs, jax.ShapeDtypeStruct((8, 128), I32)), [pltpu.VM...  7.08 us
    pallas_call x1, Pallas kernels, on_device(): call(unroute_kernel, shaped(NZ, COLUMNS), [pltpu.VMEM((16, COLUMNS + 256)...  5.06 us

commit v1 on v0

v1 whole, which is shorter than its diff:
```python
import functools

import jax
import jax.numpy as jnp
from jax import lax
from jax.experimental import pallas as pl
from jax.experimental.pallas import tpu as pltpu
from jax.sharding import PartitionSpec as P

MESH = pl.DeviceIdType.MESH
F32, BF16, I32 = jnp.float32, jnp.bfloat16, jnp.int32

NZ = 10
CX = 32
CY = 256
GX = 16
GY = 8
DEVICES = GX * GY
GROUP = 16
GROUPS = DEVICES // GROUP
COLUMNS = CX * CY
HALO = 8
ROWS = CX + 2 * HALO
LANES = CY + 128
OMEGA = 0.8
VMEM_LIMIT = 56 * 1024 * 1024

VMEM = pl.BlockSpec(memory_space=pltpu.VMEM)
SMEM = pl.BlockSpec(memory_space=pltpu.SMEM)


def iota(shape, dim):
    return lax.broadcasted_iota(I32, shape, dim)


def params(**extra):
    return pltpu.CompilerParams(vmem_limit_bytes=VMEM_LIMIT, **extra)


def owner_ends(block_ref, row):
    owners = iota((DEVICES, 128), 0)

    def count(j, total):
        piece = block_ref[:, pl.ds(pl.multiple_of(j * 128, 128), 128)]
        return total + jnp.where(piece <= owners, 1.0, 0.0)

    total = lax.fori_loop(0, COLUMNS // 128, count, jnp.zeros((DEVICES, 128), F32), unroll=4)
    row[...] = lax.dot_general(
        jnp.ones((8, 128), BF16), total.astype(BF16), (((1,), (1,)), ((), ())), preferred_element_type=F32
    ).astype(I32)


def column_fluxes(cell_ref, precip_ref, evap_ref, root_ref, sat_ref, payload):
    width = 512

    def chunk(j, carry):
        at = pl.ds(pl.multiple_of(j * width, width), width)
        sat = sat_ref[:, at]
        weights = root_ref[:, at] * sat * sat
        total = 0.25 + jnp.sum(weights, axis=0, keepdims=True)
        uptake = evap_ref[:, at] * weights / total
        top = sat[0:1]
        infiltration = precip_ref[:, at] * (1.0 - top * top * top)
        payload[0:NZ, at] = jnp.where(iota((NZ, width), 0) == 0, infiltration, 0.0) - uptake
        payload[NZ : NZ + 1, at] = cell_ref[:, at].astype(F32)
        return carry

    lax.fori_loop(0, COLUMNS // width, chunk, 0)
    payload[:, COLUMNS : COLUMNS + 256] = jnp.zeros((16, 256), F32)


def run_of(ends, owner):
    end = ends[0, owner]
    start = jnp.where(owner == 0, 0, ends[0, jnp.maximum(owner - 1, 0)])
    base = pl.multiple_of((start // 128) * 128, 128)
    return start, end, base, start - base


def prep_kernel(block_ref, cell_ref, precip_ref, evap_ref, root_ref, sat_ref, messages_ref, ends_ref, payload, ends, sem):
    owner_ends(block_ref, ends_ref)
    copy = pltpu.make_async_copy(ends_ref, ends, sem)
    copy.start()
    column_fluxes(cell_ref, precip_ref, evap_ref, root_ref, sat_ref, payload)
    copy.wait()
    lane = iota((16, 128), 1)
    row = iota((16, 128), 0)

    def one(owner, carry):
        start, end, base, shift = run_of(ends, owner)
        amount = jnp.where(shift == 0, 0, 128 - shift)
        first = pltpu.roll(payload[:, pl.ds(base, 128)], amount, 1)
        second = pltpu.roll(payload[:, pl.ds(pl.multiple_of(base + 128, 128), 128)], amount, 1)
        slab = jnp.where(lane < 128 - shift, first, second)
        messages_ref[owner] = jnp.where((row == NZ) & (lane >= end - start), -1.0, slab)
        return carry

    lax.fori_loop(0, DEVICES, one, 0, unroll=4)


def unroute_kernel(ends, answer_ref, out_ref, wide):
    lane = iota((16, 128), 1)

    def one(owner, carry):
        _, _, base, shift = run_of(ends, owner)
        slab = pltpu.roll(answer_ref[owner], shift, 1)
        here = pl.ds(base, 128)
        wide[:, here] = jnp.where(lane >= shift, slab, wide[:, here])
        wide[:, pl.ds(pl.multiple_of(base + 128, 128), 128)] = slab
        return carry

    lax.fori_loop(0, DEVICES, one, 0, unroll=4)
    out_ref[...] = wide[0:NZ, 0:COLUMNS]


def position():
    return lax.axis_index("gx"), lax.axis_index("gy")


def device_at(offset):
    gx, gy = position()
    flat = lax.rem(gx * GY + gy + offset, DEVICES)
    return flat // GY, lax.rem(flat, GY)


def neighbour(dx, dy):
    gx, gy = position()
    return lax.rem(gx + dx + GX, GX), lax.rem(gy + dy + GY, GY)


def greet_all():
    barrier = pltpu.get_barrier_semaphore()

    def greet(k, carry):
        pl.semaphore_signal(barrier, inc=1, device_id=device_at(k), device_id_type=MESH)
        return carry

    lax.fori_loop(1, DEVICES, greet, 0)


def send_messages(messages, incoming, send_sem, recv_sems):
    def send(k, carry):
        to = device_at(k)
        pltpu.make_async_remote_copy(
            src_ref=messages.at[to[0] * GY + to[1], pl.ds(0, NZ + 1)],
            dst_ref=incoming.at[k, pl.ds(0, NZ + 1)],
            send_sem=send_sem,
            recv_sem=recv_sems.at[k // GROUP],
            device_id=to,
            device_id_type=MESH,
        ).start()
        return carry

    lax.fori_loop(1, DEVICES, send, 0)
    gx, gy = position()
    incoming[0] = messages[gx * GY + gy]


def wait_for(ref, first, count, rows, sem):
    part = ref.at[pl.ds(first, count), pl.ds(0, rows)]
    pltpu.make_async_copy(part, part, sem).wait()


def send_replies(reply, answer, first, last, send_sem, recv_sem):
    gx, gy = position()
    me = gx * GY + gy

    def send(k, carry):
        pltpu.make_async_remote_copy(
            src_ref=reply.at[k, pl.ds(0, NZ)],
            dst_ref=answer.at[me, pl.ds(0, NZ)],
            send_sem=send_sem,
            recv_sem=recv_sem,
            device_id=device_at(DEVICES - k),
            device_id_type=MESH,
        ).start()
        return carry

    lax.fori_loop(first, last, send, 0)


SIDES = tuple((dx, dy) for dx in (-1, 0, 1) for dy in (-1, 0, 1) if (dx, dy) != (0, 0))


def halo_copies(block, strips, x_halo, y_halo, send_sem, recv_sem):
    copies = []
    for at, (dx, dy) in enumerate(SIDES):
        from_rows = {-1: pl.ds(0, HALO), 0: pl.ds(0, CX), 1: pl.ds(CX - HALO, HALO)}[dx]
        to_rows = {-1: pl.ds(ROWS - HALO, HALO), 0: pl.ds(HALO, CX), 1: pl.ds(0, HALO)}[dx]
        if dy == 0:
            source, target = block.at[:, :, from_rows, :], x_halo.at[0 if dx == 1 else 1]
        else:
            source = strips.at[0 if dy == -1 else 1, :, from_rows, :]
            target = y_halo.at[0 if dy == 1 else 1, :, to_rows, :]
        copies.append(
            pltpu.make_async_remote_copy(
                src_ref=source,
                dst_ref=target,
                send_sem=send_sem.at[at],
                recv_sem=recv_sem.at[at],
                device_id=neighbour(dx, dy),
                device_id_type=MESH,
            )
        )
    return copies


def pack_strips(block, at, strips):
    group = iota((CX, 128), 1) // HALO
    low = jnp.zeros((CX, 128), F32)
    high = jnp.zeros((CX, 128), F32)
    for k in range(NZ):
        low = jnp.where(group == k, pltpu.roll(block[at, k, :, 0:128], HALO * k, 1), low)
        high = jnp.where(group == k, pltpu.roll(block[at, k, :, CY - 128 : CY], HALO * (k + 1), 1), high)
    strips[0, at] = low
    strips[1, at] = high


def make_block(pressure_ref, conductivity_ref, porosity_ref, freeze_ref, block, strips):
    for k in range(NZ):
        freeze = freeze_ref[k]
        factor = jnp.where(freeze == 0, 1.0, jnp.where(freeze == 1, 0.2, 0.02)).astype(F32)
        block[0, k] = conductivity_ref[k] * factor
        block[1, k] = porosity_ref[k]
        block[2, k] = pressure_ref[k]
    for at in range(3):
        pack_strips(block, at, strips)


def widen(block, at, x_halo, y_halo, wide):
    lane = iota((ROWS, 128), 1)
    for k in range(NZ):
        wide[k, HALO : HALO + CX, 0:CY] = block[at, k]
        wide[k, 0:HALO, 0:CY] = x_halo[0, at, k]
        wide[k, HALO + CX : ROWS, 0:CY] = x_halo[1, at, k]
        low = pltpu.roll(y_halo[0, at], 120 - HALO * k, 1)
        high = pltpu.roll(y_halo[1, at], (128 - HALO * k) % 128, 1)
        wide[k, :, CY:LANES] = jnp.where(lane < HALO, high, jnp.where(lane >= 128 - HALO, low, 0.0))


def compact(ref, group):
    lane = iota((16, 128), 1)
    first, second, third, fourth = (ref[group * 4 + i] for i in range(4))
    second = pltpu.roll(second, 96, 1)
    third = pltpu.roll(third, 64, 1)
    fourth = pltpu.roll(fourth, 32, 1)
    return (
        jnp.where(lane < 96, first, second),
        jnp.where(lane < 64, second, third),
        jnp.where(lane < 32, third, fourth),
    )


def places(tile):
    cell = tile[NZ : NZ + 1].astype(I32)
    return cell >> 8, cell & (CY - 1)


def hot(index, size):
    rows = iota((size, index.shape[1]), 0).astype(F32).astype(BF16)
    marks = jnp.broadcast_to(index.astype(F32), (16, index.shape[1])).astype(BF16)
    marks = jnp.concatenate([marks] * (size // 16), axis=0)
    return jnp.where(rows == marks, jnp.ones((), BF16), jnp.zeros((), BF16))


def scatter_group(incoming, group, total):
    tiles = ()
    for i in range(GROUP // 4):
        tiles = tiles + compact(incoming, group * (GROUP // 4) + i)
    high_parts, low_parts, right_parts = [], [], []
    for tile in tiles:
        at_x, at_y = places(tile)
        hot_x = hot(at_x, CX)
        high = tile.astype(BF16).astype(F32)
        low = tile - high
        for part, into in ((high, high_parts), (low, low_parts)):
            rows = []
            for k in range(NZ):
                spread = jnp.broadcast_to(part[k : k + 1], (16, 128)).astype(BF16)
                rows += [spread * hot_x[0:16], spread * hot_x[16:32]]
            into.append(jnp.concatenate(rows, axis=0))
        right_parts.append(hot(at_y, CY))
    left = jnp.concatenate(high_parts + low_parts, axis=1)
    right = jnp.concatenate(right_parts + right_parts, axis=1)
    total[...] += lax.dot_general(left, right, (((1,), (1,)), ((), ())), preferred_element_type=F32)


def keep_source(total, mask_ref, source, strips):
    mask = mask_ref[...].astype(F32)
    for k in range(NZ):
        source[0, k] = total[k * CX : (k + 1) * CX] * mask
    pack_strips(source, 0, strips)


def up(field, dim):
    return pltpu.roll(field, field.shape[dim] - 1, dim)


def down(field, dim):
    return pltpu.roll(field, 1, dim)


def dry_inverse(field):
    dryness = jnp.maximum(-field, 0.0)
    return dryness, lax.rsqrt(1.0 + dryness * dryness)


def joined(one, two):
    both = one + two
    return one * two / jnp.where(both > 0.0, both, 1.0)


def grid_edges(wide_shape):
    gx, gy = position()
    row, lane = iota(wide_shape, 0), iota(wide_shape, 1)
    outside = ((row < HALO) & (gx == 0)) | ((row >= HALO + CX) & (gx == GX - 1))
    return outside | ((lane >= CY + 64) & (gy == 0)) | ((lane >= CY) & (lane < CY + 64) & (gy == GY - 1))


def zero_ends(p, kr, gz, u, v):
    zero = jnp.zeros((ROWS, LANES), F32)
    for ref, at in ((p, NZ), (kr, NZ), (gz, 0), (gz, NZ), (u, 0), (u, NZ + 1), (v, 0), (v, NZ + 1)):
        ref[at] = zero


def make_faces(perm, p, stored, hx, hy, hz):
    outside = grid_edges((ROWS, LANES))

    def prepare(k, carry):
        perm[k] = jnp.where(outside, 0.0, perm[k])
        return carry

    lax.fori_loop(0, NZ, prepare, 0)

    def faces(k, carry):
        here = perm[k]
        hx[k] = joined(here, up(here, 0))
        hy[k] = joined(here, up(here, 1))
        stored[k] = dry_inverse(p[k])[1]
        return carry

    lax.fori_loop(0, NZ, faces, 0)

    def vertical_faces(k, carry):
        hz[k] = joined(perm[k], perm[k + 1])
        return carry

    lax.fori_loop(0, NZ - 1, vertical_faces, 0)


def linearize(perm, porosity, p, stored, kr, hx, hy, hz, gx_, gy_, gz, scale, start):
    def relative(k, carry):
        inverse = dry_inverse(p[k])[1]
        kr[k] = inverse * inverse * inverse
        return carry

    lax.fori_loop(0, NZ, relative, 0)

    def layer(k, flow_above, last):
        here, rel = p[k], kr[k]
        side_x = hx[k] * (rel + up(rel, 0))
        side_y = hy[k] * (rel + up(rel, 1))
        gx_[k] = side_x
        gy_[k] = side_y
        flow_x = side_x * (here - up(here, 0))
        flow_y = side_y * (here - up(here, 1))
        above = gz[k]
        if last:
            flow = perm[k] * rel
        else:
            below = hz[k] * (rel + kr[k + 1])
            gz[k + 1] = below
            flow = below * (here - p[k + 1] + 1.0)
        dryness, inverse = dry_inverse(here)
        residual = porosity[k] * (inverse - stored[k]) + (flow_x - down(flow_x, 0)) + (flow_y - down(flow_y, 1))
        start[k] = residual + flow - flow_above
        diagonal = porosity[k] * (dryness * rel) + side_x + down(side_x, 0) + side_y + down(side_y, 1) + above
        if not last:
            diagonal = diagonal + below
        scale[k] = OMEGA / jnp.where(diagonal > 0.0, diagonal, 1.0)
        return flow

    flow = lax.fori_loop(0, NZ - 1, lambda k, f: layer(k, f, False), jnp.zeros((ROWS, LANES), F32))
    layer(NZ - 1, flow, True)


def smooth(p, src, gx_, gy_, gz, scale, start, u, v):
    def first(k, carry):
        opening = (src[k] - start[k]) * scale[k]
        start[k] = opening
        u[k + 1] = opening
        return carry

    lax.fori_loop(0, NZ, first, 0)
    for old, new in ((u, v), (v, u), (u, v)):

        def sweep(k, carry, old=old, new=new):
            here = old[k + 1]
            side_x, side_y = gx_[k], gy_[k]
            coupled = side_x * up(here, 0) + down(side_x * here, 0) + side_y * up(here, 1) + down(side_y * here, 1)
            coupled = coupled + gz[k] * old[k] + gz[k + 1] * old[k + 2]
            new[k + 1] = (1.0 - OMEGA) * here + start[k] + scale[k] * coupled
            return carry

        lax.fori_loop(0, NZ, sweep, 0)

    def advance(k, carry):
        p[k] = p[k] + v[k + 1]
        return carry

    lax.fori_loop(0, NZ, advance, 0)


def finish(p, pressure_out, saturated):
    for k in range(NZ):
        final = p[k, HALO : HALO + CX, 0:CY]
        pressure_out[k] = final
        rows = pl.ds(k, CX, stride=8) if k < 8 else pl.ds(CX * 8 + k - 8, CX, stride=2)
        sat = dry_inverse(final)[1]
        saturated[0, rows, :] = sat[:, 0:128]
        saturated[1, rows, :] = sat[:, 128:256]


def gather_group(saturated, incoming, group, reply):
    lane = iota((16, 128), 1)
    row = iota((8, 128), 0)
    every = jnp.concatenate([saturated[0], saturated[1]], axis=1)
    high = every.astype(BF16)
    left = jnp.concatenate([high, (every - high.astype(F32)).astype(BF16)], axis=1)
    for pair in range(GROUP // 8):
        at = group * (GROUP // 4) + 2 * pair
        tiles = compact(incoming, at) + compact(incoming, at + 1)
        spots = [places(tile) for tile in tiles]
        outs = []
        for i in range(3):
            two = jnp.concatenate([hot(spots[2 * i][1], CY), hot(spots[2 * i + 1][1], CY)], axis=1)
            both = jnp.concatenate([two, two], axis=0)
            lines = jnp.dot(left, both, preferred_element_type=F32)
            for half in range(2):
                part = lines[:, half * 128 : half * 128 + 128]
                at_x = jnp.broadcast_to(spots[2 * i + half][0], (8, 128))
                first = part[0:8]
                for x in range(1, CX):
                    first = jnp.where(at_x == x, part[8 * x : 8 * x + 8], first)
                second = part[256:264]
                for g in range(1, 8):
                    second = jnp.where((at_x >> 2) == g, part[256 + 8 * g : 264 + 8 * g], second)
                second = jnp.where((row >> 1) == (at_x & 3), second, 0.0)
                second = second + pltpu.roll(second, 4, 0)
                second = second + pltpu.roll(second, 2, 0)
                outs.append(jnp.concatenate([first, second], axis=0))
        for j in range(2):
            one, two, three = outs[3 * j : 3 * j + 3]
            base = group * GROUP + pair * 8 + j * 4
            reply[base] = one
            reply[base + 1] = pltpu.roll(jnp.where(lane >= 96, one, two), 32, 1)
            reply[base + 2] = pltpu.roll(jnp.where(lane >= 64, two, three), 64, 1)
            reply[base + 3] = pltpu.roll(three, 96, 1)


def interval_kernel(
    messages, pressure_ref, conductivity_ref, porosity_ref, freeze_ref, mask_ref, pressure_out, answer,
    incoming, reply, saturated, total, block, strips, x_halo, y_halo, source, source_strips, source_x, source_y,
    perm, porosity, p, src, stored, kr, hx, hy, hz, gx_, gy_, gz, scale, start, u, v,
    sems, group_sems, halo_send, halo_recv, source_send, source_recv,
):
    greet_all()
    make_block(pressure_ref, conductivity_ref, porosity_ref, freeze_ref, block, strips)
    pl.semaphore_wait(pltpu.get_barrier_semaphore(), DEVICES - 1)
    halos = halo_copies(block, strips, x_halo, y_halo, halo_send, halo_recv)
    for copy in halos:
        copy.start()
    send_messages(messages, incoming, sems.at[0], group_sems)
    zero_ends(p, kr, gz, u, v)
    total[...] = jnp.zeros_like(total)
    for copy in halos:
        copy.wait_recv()
    widen(block, 0, x_halo, y_halo, perm)
    widen(block, 1, x_halo, y_halo, porosity)
    widen(block, 2, x_halo, y_halo, p)
    make_faces(perm, p, stored, hx, hy, hz)
    linearize(perm, porosity, p, stored, kr, hx, hy, hz, gx_, gy_, gz, scale, start)
    wait_for(incoming, 1, GROUP - 1, NZ + 1, group_sems.at[0])
    scatter_group(incoming, 0, total)

    def arrive(group, carry):
        wait_for(incoming, group * GROUP, GROUP, NZ + 1, group_sems.at[group])
        scatter_group(incoming, group, total)
        return carry

    lax.fori_loop(1, GROUPS, arrive, 0)
    keep_source(total, mask_ref, source, source_strips)
    copies = halo_copies(source, source_strips, source_x, source_y, source_send, source_recv)
    for copy in copies:
        copy.start()
    for copy in copies:
        copy.wait_recv()
    widen(source, 0, source_x, source_y, src)
    smooth(p, src, gx_, gy_, gz, scale, start, u, v)
    linearize(perm, porosity, p, stored, kr, hx, hy, hz, gx_, gy_, gz, scale, start)
    smooth(p, src, gx_, gy_, gz, scale, start, u, v)
    finish(p, pressure_out, saturated)
    gather_group(saturated, incoming, 0, reply)
    send_replies(reply, answer, 1, GROUP, sems.at[1], sems.at[2])
    gx, gy = position()
    answer[gx * GY + gy] = reply[0]

    def depart(group, carry):
        gather_group(saturated, incoming, group, reply)
        send_replies(reply, answer, group * GROUP, group * GROUP + GROUP, sems.at[1], sems.at[2])
        return carry

    lax.fori_loop(1, GROUPS, depart, 0)
    for copy in halos + copies:
        copy.wait_send()
    wait_for(messages, 1, DEVICES - 1, NZ + 1, sems.at[0])
    wait_for(reply, 1, DEVICES - 1, NZ, sems.at[1])
    wait_for(answer, 1, DEVICES - 1, NZ, sems.at[2])


def shaped(*lengths):
    return jax.ShapeDtypeStruct(lengths, F32)


def call(kernel, outs, scratch, extra=None, ins=None, count=None):
    return pl.pallas_call(
        kernel,
        out_shape=outs,
        in_specs=ins or [VMEM] * count,
        out_specs=jax.tree.map(lambda _: VMEM, outs),
        scratch_shapes=scratch,
        compiler_params=params(**(extra or {})),
    )


def on_device(
    clm_block, clm_cell, precip, evap_demand, root_share, sat_before,
    pressure, conductivity, porosity, freeze_state, land_mask,
):
    flat = [a.reshape(1, COLUMNS) for a in (clm_block, clm_cell, precip, evap_demand)]
    slabs = shaped(DEVICES, 16, 128)
    dma = pltpu.SemaphoreType.DMA
    messages, ends = call(
        prep_kernel,
        (slabs, jax.ShapeDtypeStruct((8, 128), I32)),
        [pltpu.VMEM((16, COLUMNS + 256), F32), pltpu.SMEM((8, 128), I32), dma],
        count=6,
    )(*flat, root_share, sat_before)
    wide = [
        pltpu.VMEM((n, ROWS, LANES), F32)
        for n in (NZ, NZ, NZ + 1, NZ, NZ, NZ + 1, NZ, NZ, NZ, NZ, NZ, NZ + 1, NZ, NZ, NZ + 2, NZ + 2)
    ]
    memory = lambda *lengths: pltpu.VMEM(lengths, F32)
    new_pressure, answer = call(
        interval_kernel,
        (shaped(NZ, CX, CY), slabs),
        [memory(DEVICES, 16, 128), memory(DEVICES, 16, 128), memory(2, NZ * CX, 128), memory(NZ * CX, CY)]
        + [memory(3, NZ, CX, CY), memory(2, 3, CX, 128), memory(2, 3, NZ, HALO, CY), memory(2, 3, ROWS, 128)]
        + [memory(1, NZ, CX, CY), memory(2, 1, CX, 128), memory(2, 1, NZ, HALO, CY), memory(2, 1, ROWS, 128)]
        + wide
        + [dma((3,)), dma((GROUPS,)), dma((8,)), dma((8,)), dma((8,)), dma((8,))],
        dict(collective_id=0, has_side_effects=True),
        count=6,
    )(messages, pressure, conductivity, porosity, freeze_state, land_mask)
    returned = call(
        unroute_kernel, shaped(NZ, COLUMNS), [pltpu.VMEM((16, COLUMNS + 256), F32)], ins=[SMEM, VMEM]
    )(ends, answer)
    return new_pressure, returned


def solution(mesh):
    both = P(("gx", "gy"))
    columns = P(None, ("gx", "gy"))
    grid = P(None, "gx", "gy")
    return jax.shard_map(
        on_device,
        mesh=mesh,
        in_specs=(both, both, both, both, columns, columns, grid, grid, grid, grid, P("gx", "gy")),
        out_specs=(grid, columns),
        check_vma=False,
    )
```

time: 125 us -> 83.2 us (0.67)
  Pallas kernels: 124 us -> 81.6 us
    pallas_call x6 -> x1, Pallas kernels: 112 us -> 69.4 us  [on_device(): call(interval_kernel, (shaped(NZ, CX, CY), slabs), [memory(DEVICES, 16, 1...]
where the time goes in v1:
time: 83.2 us; the launch traced here: 83 us
  Pallas kernels  81.6 us (98%)
    pallas_call x1, Pallas kernels, on_device(): call(interval_kernel, (shaped(NZ, CX, CY), slabs), [memory(DEVICES, 16, 1...  69.4 us
    pallas_call x1, Pallas kernels, on_device(): call(prep_kernel, (slabs, jax.ShapeDtypeStruct((8, 128), I32)), [pltpu.VM...  7.03 us
    pallas_call x1, Pallas kernels, on_device(): call(unroute_kernel, shaped(NZ, COLUMNS), [pltpu.VMEM((16, COLUMNS + 256)...  5.11 us

profile of v1, /device:TPU:1, one launch (start us, length us, event | category | flops | bytes accessed | tf_op | source)
XLA Modules:
  0.0 83.0 jit_solution(7773603204839980460)
XLA Ops:
  0.6 7.0 %shard_map.122 = (f32[128,16,128]{2,1,0:T(8,128)}, s32[8,128]{1,0:T(8,128)}) custom-call(s32[1,8192]{1,0:T(1,128)} %bitcast.4, s32[1,8192]{1,0:T(1,128)} %bitcast.5, f32[1,8192]{1,0:T(1,128)} %bitcast.6, f32[1,8192]{1,0:T(1,128)} %bitcast.7, f32[10,8192]{1,0:T(8,128)} %root_ref.1, f32[10,8192]{1,0:T(8,128)} %sat_ref.1), custom_call_target="tpu_custom_call" | custom-call | tf_op jit(solution)/shard_map/pallas_call | solution.py:542
  7.7 69.4 %shard_map.123 = (f32[10,32,256]{2,1,0:T(8,128)}, f32[128,16,128]{2,1,0:T(8,128)}) custom-call(f32[128,16,128]{2,1,0:T(8,128)} %get-tuple-element.6.messages, f32[10,32,256]{2,1,0:T(8,128)} %pressure_ref.1, f32[10,32,256]{2,1,0:T(8,128)} %conductivity_ref.1, f32[10,32,256]{2,1,0:T(8,128)} %porosity_ref.1, s32[10,32,256]{2,1,0:T(8,128)} %freeze_ref.1, ...), custom_call_target="tpu_custom_call" | custom-call | tf_op jit(solution)/shard_map/pallas_call | solution.py:553
  77.1 0.0 copy-start
  77.1 5.1 %shard_map.124 = f32[10,8192]{1,0:T(8,128)} custom-call(s32[8,128]{1,0:T(8,128)} %get-tuple-element.8.ends, f32[128,16,128]{2,1,0:T(8,128)} %get-tuple-element.9.answer_ref), custom_call_target="tpu_custom_call" | custom-call | tf_op jit(solution)/shard_map/pallas_call | solution.py:564
  82.2 0.0 copy-done
  82.2 0.7 copy.14
Async XLA Ops:
  77.1 5.1 %copy-start = (f32[10,32,256]{2,1,0:T(8,128)S(1)}, f32[10,32,256]{2,1,0:T(8,128)}, u32[]{:S(2)}) copy-start(f32[10,32,256]{2,1,0:T(8,128)} %get-tuple-element.12) | copy-start | bytes 983044

commit v2 on v1

--- a/solution.py
+++ b/solution.py
@@ -18,6 +18,7 @@
 DEVICES = GX * GY
 GROUP = 16
 GROUPS = DEVICES // GROUP
+SENT = 9
 COLUMNS = CX * CY
 HALO = 8
 ROWS = CX + 2 * HALO
@@ -42,12 +43,10 @@
 
     def count(j, total):
         piece = block_ref[:, pl.ds(pl.multiple_of(j * 128, 128), 128)]
-        return total + jnp.where(piece <= owners, 1.0, 0.0)
-
-    total = lax.fori_loop(0, COLUMNS // 128, count, jnp.zeros((DEVICES, 128), F32), unroll=4)
-    row[...] = lax.dot_general(
-        jnp.ones((8, 128), BF16), total.astype(BF16), (((1,), (1,)), ((), ())), preferred_element_type=F32
-    ).astype(I32)
+        return total + jnp.where(piece <= owners, 1, 0)
+
+    total = lax.fori_loop(0, COLUMNS // 128, count, jnp.zeros((DEVICES, 128), I32), unroll=4)
+    row[...] = jnp.broadcast_to(jnp.sum(total.T, axis=0, keepdims=True), (8, 128))
 
 
 def column_fluxes(cell_ref, precip_ref, evap_ref, root_ref, sat_ref, payload):
@@ -69,6 +68,28 @@
     payload[:, COLUMNS : COLUMNS + 256] = jnp.zeros((16, 256), F32)
 
 
+def fold_last_rows(payload, folded):
+    row, lane = iota((8, 128), 0), iota((8, 128), 1)
+    third = jnp.where(row >= 6, row - 6, jnp.where(row >= 3, row - 3, row))
+    moved = 96 - 32 * third
+
+    def tile(t, carry):
+        before, before_last = carry
+        at = pl.ds(pl.multiple_of(t * 128, 128), 128)
+        rows = [jnp.broadcast_to(payload[k : k + 1, at], (8, 128)) for k in (8, 9, 10)]
+        mixed = jnp.where(row < 3, rows[0], jnp.where(row < 6, rows[1], rows[2]))
+        here = jnp.where(
+            third == 0, pltpu.roll(mixed, 96, 1), jnp.where(third == 1, pltpu.roll(mixed, 64, 1), pltpu.roll(mixed, 32, 1))
+        )
+        last = pltpu.roll(rows[2], 32, 1)
+        folded[0:8, at] = jnp.where(lane < moved, before, here)
+        folded[8:16, at] = jnp.where(lane < 32, before_last, last)
+        return here, last
+
+    zero = jnp.zeros((8, 128), F32)
+    lax.fori_loop(0, COLUMNS // 128 + 2, tile, (zero, zero), unroll=22)
+
+
 def run_of(ends, owner):
     end = ends[0, owner]
     start = jnp.where(owner == 0, 0, ends[0, jnp.maximum(owner - 1, 0)])
@@ -76,40 +97,78 @@
     return start, end, base, start - base
 
 
-def prep_kernel(block_ref, cell_ref, precip_ref, evap_ref, root_ref, sat_ref, messages_ref, ends_ref, payload, ends, sem):
-    owner_ends(block_ref, ends_ref)
-    copy = pltpu.make_async_copy(ends_ref, ends, sem)
-    copy.start()
-    column_fluxes(cell_ref, precip_ref, evap_ref, root_ref, sat_ref, payload)
-    copy.wait()
-    lane = iota((16, 128), 1)
-    row = iota((16, 128), 0)
+def make_messages(ends, payload, folded, messages):
+    lane, row = iota((8, 128), 1), iota((8, 128), 0)
+    place = jnp.where(lane >= 96, lane - 96 + 32 * (row - 6), 0)
+    cells = (lane >= 96) & (row >= 6)
 
     def one(owner, carry):
         start, end, base, shift = run_of(ends, owner)
         amount = jnp.where(shift == 0, 0, 128 - shift)
-        first = pltpu.roll(payload[:, pl.ds(base, 128)], amount, 1)
-        second = pltpu.roll(payload[:, pl.ds(pl.multiple_of(base + 128, 128), 128)], amount, 1)
+        here, there = pl.ds(base, 128), pl.ds(pl.multiple_of(base + 128, 128), 128)
+        cut = shift + 96
+        first = pltpu.roll(jnp.where(lane < cut, payload[0:8, here], folded[0:8, here]), amount, 1)
+        second = pltpu.roll(jnp.where(lane + 128 < cut, payload[0:8, there], folded[0:8, there]), amount, 1)
         slab = jnp.where(lane < 128 - shift, first, second)
-        messages_ref[owner] = jnp.where((row == NZ) & (lane >= end - start), -1.0, slab)
-        return carry
-
-    lax.fori_loop(0, DEVICES, one, 0, unroll=4)
-
-
-def unroute_kernel(ends, answer_ref, out_ref, wide):
-    lane = iota((16, 128), 1)
+        messages[owner, 0:8] = jnp.where(cells & (place >= end - start), -1.0, slab)
+        first = pltpu.roll(folded[8:16, here], amount, 1)
+        second = pltpu.roll(folded[8:16, there], amount, 1)
+        slab = jnp.where(lane < 128 - shift, first, second)
+        messages[owner, 8:16] = jnp.where(lane - 32 >= end - start, -1.0, slab)
+        return carry
+
+    lax.fori_loop(0, DEVICES, one, 0, unroll=16)
+
+
+def prep_kernel(*refs):
+    given, (messages, ends_out), held = refs[:6], refs[6:8], refs[8:14]
+    payload, folded, ends, load_sems, ends_sem = refs[14:]
+    loads = [pltpu.make_async_copy(one, kept, load_sems.at[i]) for i, (one, kept) in enumerate(zip(given, held))]
+    for load in loads:
+        load.start()
+    loads[0].wait()
+    owner_ends(held[0], ends_out)
+    copy_ends = pltpu.make_async_copy(ends_out, ends, ends_sem)
+    copy_ends.start()
+    for load in loads[1:]:
+        load.wait()
+    column_fluxes(*held[1:], payload)
+    fold_last_rows(payload, folded)
+    copy_ends.wait()
+    make_messages(ends, payload, folded, messages)
+
+
+def unroute_kernel(ends, answer_ref, pressure_ref, pressure_out, out_ref, wide, wide_last, last):
+    pressure_out[...] = pressure_ref[...]
+    lane = iota((DEVICES, 128), 1)
+    for k in range(2):
+        thirds = [
+            pltpu.roll(answer_ref[pl.ds(2 * third + k, DEVICES, stride=8), :], 32 * (third + 1), 1) for third in range(3)
+        ]
+        last[pl.ds(k, DEVICES, stride=8), :] = jnp.where(
+            lane < 32, thirds[0], jnp.where(lane < 64, thirds[1], thirds[2])
+        )
+    lane = iota((8, 128), 1)
 
     def one(owner, carry):
+        tile, tile_last, before, before_last, old = carry
         _, _, base, shift = run_of(ends, owner)
-        slab = pltpu.roll(answer_ref[owner], shift, 1)
-        here = pl.ds(base, 128)
-        wide[:, here] = jnp.where(lane >= shift, slab, wide[:, here])
-        wide[:, pl.ds(pl.multiple_of(base + 128, 128), 128)] = slab
-        return carry
-
-    lax.fori_loop(0, DEVICES, one, 0, unroll=4)
-    out_ref[...] = wide[0:NZ, 0:COLUMNS]
+        at = pl.ds(pl.multiple_of(owner * 8, 8), 8)
+        slab = pltpu.roll(answer_ref[at, :], shift, 1)
+        slab_last = pltpu.roll(last[at, :], shift, 1)
+        here, there = pl.ds(base, 128), pl.ds(pl.multiple_of(base + 128, 128), 128)
+        tile = jnp.where(lane >= shift, slab, jnp.where(base == old, tile, before))
+        tile_last = jnp.where(lane >= shift, slab_last, jnp.where(base == old, tile_last, before_last))
+        wide[:, here] = tile
+        wide_last[:, here] = tile_last
+        wide[:, there] = slab
+        wide_last[:, there] = slab_last
+        return tile, tile_last, slab, slab_last, base
+
+    zero = jnp.zeros((8, 128), F32)
+    lax.fori_loop(0, DEVICES, one, (zero, zero, zero, zero, jnp.int32(0)), unroll=16)
+    out_ref[0:8, :] = wide[:, 0:COLUMNS]
+    out_ref[8:NZ, :] = wide_last[0:2, 0:COLUMNS]
 
 
 def position():
@@ -137,22 +196,20 @@
     lax.fori_loop(1, DEVICES, greet, 0)
 
 
-def send_messages(messages, incoming, send_sem, recv_sems):
+def send_messages(messages, incoming, group, send_sem, recv_sems):
     def send(k, carry):
         to = device_at(k)
         pltpu.make_async_remote_copy(
-            src_ref=messages.at[to[0] * GY + to[1], pl.ds(0, NZ + 1)],
-            dst_ref=incoming.at[k, pl.ds(0, NZ + 1)],
+            src_ref=messages.at[to[0] * GY + to[1], pl.ds(0, SENT)],
+            dst_ref=incoming.at[k, pl.ds(0, SENT)],
             send_sem=send_sem,
-            recv_sem=recv_sems.at[k // GROUP],
+            recv_sem=recv_sems.at[group],
             device_id=to,
             device_id_type=MESH,
         ).start()
         return carry
 
-    lax.fori_loop(1, DEVICES, send, 0)
-    gx, gy = position()
-    incoming[0] = messages[gx * GY + gy]
+    lax.fori_loop(max(group * GROUP, 1), (group + 1) * GROUP, send, 0)
 
 
 def wait_for(ref, first, count, rows, sem):
@@ -166,8 +223,8 @@
 
     def send(k, carry):
         pltpu.make_async_remote_copy(
-            src_ref=reply.at[k, pl.ds(0, NZ)],
-            dst_ref=answer.at[me, pl.ds(0, NZ)],
+            src_ref=reply.at[k, pl.ds(0, 8)],
+            dst_ref=answer.at[me, pl.ds(0, 8)],
             send_sem=send_sem,
             recv_sem=recv_sem,
             device_id=device_at(DEVICES - k),
@@ -238,20 +295,32 @@
 
 
 def compact(ref, group):
-    lane = iota((16, 128), 1)
-    first, second, third, fourth = (ref[group * 4 + i] for i in range(4))
+    lane = iota((8, 128), 1)
+    first, second, third, fourth = (ref[group * 4 + i, 0:8] for i in range(4))
     second = pltpu.roll(second, 96, 1)
     third = pltpu.roll(third, 64, 1)
     fourth = pltpu.roll(fourth, 32, 1)
-    return (
+    mains = (
         jnp.where(lane < 96, first, second),
         jnp.where(lane < 64, second, third),
         jnp.where(lane < 32, third, fourth),
     )
+    quarter = iota((3, 128), 1) // 32
+    tiles = []
+    for t in range(3):
+        rest = None
+        for q in range(4):
+            at = 4 * t + q
+            piece = ref[group * 4 + at // 3, pl.ds(at % 3, 3, stride=3), :]
+            if q < 3:
+                piece = pltpu.roll(piece, 32 * (q + 1), 1)
+            rest = piece if q == 0 else jnp.where(quarter == q, piece, rest)
+        tiles.append((mains[t], rest))
+    return tuple(tiles)
 
 
 def places(tile):
-    cell = tile[NZ : NZ + 1].astype(I32)
+    cell = tile[1][2:3].astype(I32)
     return cell >> 8, cell & (CY - 1)
 
 
@@ -270,12 +339,13 @@
     for tile in tiles:
         at_x, at_y = places(tile)
         hot_x = hot(at_x, CX)
-        high = tile.astype(BF16).astype(F32)
-        low = tile - high
-        for part, into in ((high, high_parts), (low, low_parts)):
+        highs = [part.astype(BF16).astype(F32) for part in tile]
+        lows = [part - high for part, high in zip(tile, highs)]
+        for parts, into in ((highs, high_parts), (lows, low_parts)):
             rows = []
             for k in range(NZ):
-                spread = jnp.broadcast_to(part[k : k + 1], (16, 128)).astype(BF16)
+                line = parts[0][k : k + 1] if k < 8 else parts[1][k - 8 : k - 7]
+                spread = jnp.broadcast_to(line, (16, 128)).astype(BF16)
                 rows += [spread * hot_x[0:16], spread * hot_x[16:32]]
             into.append(jnp.concatenate(rows, axis=0))
         right_parts.append(hot(at_y, CY))
@@ -421,7 +491,7 @@
 
 
 def gather_group(saturated, incoming, group, reply):
-    lane = iota((16, 128), 1)
+    lane = iota((8, 128), 1)
     row = iota((8, 128), 0)
     every = jnp.concatenate([saturated[0], saturated[1]], axis=1)
     high = every.astype(BF16)
@@ -447,31 +517,67 @@
                 second = jnp.where((row >> 1) == (at_x & 3), second, 0.0)
                 second = second + pltpu.roll(second, 4, 0)
                 second = second + pltpu.roll(second, 2, 0)
-                outs.append(jnp.concatenate([first, second], axis=0))
+                outs.append((first, second))
         for j in range(2):
-            one, two, three = outs[3 * j : 3 * j + 3]
-            base = group * GROUP + pair * 8 + j * 4
-            reply[base] = one
-            reply[base + 1] = pltpu.roll(jnp.where(lane >= 96, one, two), 32, 1)
-            reply[base + 2] = pltpu.roll(jnp.where(lane >= 64, two, three), 64, 1)
-            reply[base + 3] = pltpu.roll(three, 96, 1)
-
-
-def interval_kernel(
-    messages, pressure_ref, conductivity_ref, porosity_ref, freeze_ref, mask_ref, pressure_out, answer,
-    incoming, reply, saturated, total, block, strips, x_halo, y_halo, source, source_strips, source_x, source_y,
-    perm, porosity, p, src, stored, kr, hx, hy, hz, gx_, gy_, gz, scale, start, u, v,
-    sems, group_sems, halo_send, halo_recv, source_send, source_recv,
-):
+            three = outs[3 * j : 3 * j + 3]
+            mains, rests = [m for m, _ in three], [r for _, r in three]
+            mains = (
+                mains[0],
+                pltpu.roll(jnp.where(lane >= 96, mains[0], mains[1]), 32, 1),
+                pltpu.roll(jnp.where(lane >= 64, mains[1], mains[2]), 64, 1),
+                pltpu.roll(mains[2], 96, 1),
+            )
+            for i in range(4):
+                slab = mains[i]
+                for third in range(3):
+                    at = 3 * i + third
+                    piece = rests[at // 4]
+                    if at % 4 < 3:
+                        piece = pltpu.roll(piece, 96 - 32 * (at % 4), 1)
+                    slab = jnp.where((lane >= 96) & (row >> 1 == third), piece, slab)
+                reply[group * GROUP + pair * 8 + j * 4 + i] = slab
+
+
+def interval_kernel(*refs):
+    given, (pressure_out, answer), held, refs = refs[:6], refs[6:8], refs[8:14], refs[14:]
+    (
+        incoming, reply, saturated, total, block, strips, x_halo, y_halo,
+        source, source_strips, source_x, source_y,
+        perm, porosity, p, src, stored, kr, hx, hy, hz, gx_, gy_, gz, scale, start, u, v,
+        load_sems, sems, group_sems, halo_send, halo_recv, source_send, source_recv,
+    ) = refs
+    messages, mask_ref = held[0], held[5]
+    loads = [pltpu.make_async_copy(one, kept, load_sems.at[i]) for i, (one, kept) in enumerate(zip(given, held))]
+    for load in loads[1:] + loads[:1]:
+        load.start()
     greet_all()
-    make_block(pressure_ref, conductivity_ref, porosity_ref, freeze_ref, block, strips)
+    for load in loads[1:]:
+        load.wait()
+    make_block(*held[1:5], block, strips)
+    loads[0].wait()
     pl.semaphore_wait(pltpu.get_barrier_semaphore(), DEVICES - 1)
     halos = halo_copies(block, strips, x_halo, y_halo, halo_send, halo_recv)
+    for group in range(GROUPS):
+        send_messages(messages, incoming, group, sems.at[0], group_sems)
     for copy in halos:
         copy.start()
-    send_messages(messages, incoming, sems.at[0], group_sems)
+    gx, gy = position()
+    incoming[0] = messages[gx * GY + gy]
     zero_ends(p, kr, gz, u, v)
     total[...] = jnp.zeros_like(total)
+    wait_for(incoming, 1, GROUP - 1, SENT, group_sems.at[0])
+    scatter_group(incoming, 0, total)
+
+    def arrive(group, carry):
+        wait_for(incoming, group * GROUP, GROUP, SENT, group_sems.at[group])
+        scatter_group(incoming, group, total)
+        return carry
+
+    lax.fori_loop(1, GROUPS, arrive, 0)
+    keep_source(total, mask_ref, source, source_strips)
+    copies = halo_copies(source, source_strips, source_x, source_y, source_send, source_recv)
+    for copy in copies:
+        copy.start()
     for copy in halos:
         copy.wait_recv()
     widen(block, 0, x_halo, y_halo, perm)
@@ -479,19 +585,6 @@
     widen(block, 2, x_halo, y_halo, p)
     make_faces(perm, p, stored, hx, hy, hz)
     linearize(perm, porosity, p, stored, kr, hx, hy, hz, gx_, gy_, gz, scale, start)
-    wait_for(incoming, 1, GROUP - 1, NZ + 1, group_sems.at[0])
-    scatter_group(incoming, 0, total)
-
-    def arrive(group, carry):
-        wait_for(incoming, group * GROUP, GROUP, NZ + 1, group_sems.at[group])
-        scatter_group(incoming, group, total)
-        return carry
-
-    lax.fori_loop(1, GROUPS, arrive, 0)
-    keep_source(total, mask_ref, source, source_strips)
-    copies = halo_copies(source, source_strips, source_x, source_y, source_send, source_recv)
-    for copy in copies:
-        copy.start()
     for copy in copies:
         copy.wait_recv()
     widen(source, 0, source_x, source_y, src)
@@ -512,9 +605,9 @@
     lax.fori_loop(1, GROUPS, depart, 0)
     for copy in halos + copies:
         copy.wait_send()
-    wait_for(messages, 1, DEVICES - 1, NZ + 1, sems.at[0])
-    wait_for(reply, 1, DEVICES - 1, NZ, sems.at[1])
-    wait_for(answer, 1, DEVICES - 1, NZ, sems.at[2])
+    wait_for(messages, 1, DEVICES - 1, SENT, sems.at[0])
+    wait_for(reply, 1, DEVICES - 1, 8, sems.at[1])
+    wait_for(answer, 1, DEVICES - 1, 8, sems.at[2])
 
 
 def shaped(*lengths):
@@ -537,33 +630,41 @@
     pressure, conductivity, porosity, freeze_state, land_mask,
 ):
     flat = [a.reshape(1, COLUMNS) for a in (clm_block, clm_cell, precip, evap_demand)]
-    slabs = shaped(DEVICES, 16, 128)
     dma = pltpu.SemaphoreType.DMA
-    messages, ends = call(
-        prep_kernel,
-        (slabs, jax.ShapeDtypeStruct((8, 128), I32)),
-        [pltpu.VMEM((16, COLUMNS + 256), F32), pltpu.SMEM((8, 128), I32), dma],
-        count=6,
-    )(*flat, root_share, sat_before)
     wide = [
         pltpu.VMEM((n, ROWS, LANES), F32)
         for n in (NZ, NZ, NZ + 1, NZ, NZ, NZ + 1, NZ, NZ, NZ, NZ, NZ, NZ + 1, NZ, NZ, NZ + 2, NZ + 2)
     ]
     memory = lambda *lengths: pltpu.VMEM(lengths, F32)
-    new_pressure, answer = call(
+    anywhere = pl.BlockSpec(memory_space=pl.ANY)
+    held = lambda given: [pltpu.VMEM(a.shape, a.dtype) for a in given]
+    given = (*flat, root_share, sat_before)
+    messages, ends = call(
+        prep_kernel,
+        (shaped(DEVICES, 16, 128), jax.ShapeDtypeStruct((8, 128), I32)),
+        held(given)
+        + [memory(16, COLUMNS + 256), memory(16, COLUMNS + 256), pltpu.SMEM((8, 128), I32), dma((6,)), dma],
+        ins=[anywhere] * 6,
+    )(*given)
+    given = (messages, pressure, conductivity, porosity, freeze_state, land_mask)
+    pressure_now, answer = call(
         interval_kernel,
-        (shaped(NZ, CX, CY), slabs),
-        [memory(DEVICES, 16, 128), memory(DEVICES, 16, 128), memory(2, NZ * CX, 128), memory(NZ * CX, CY)]
+        (shaped(NZ, CX, CY), shaped(DEVICES, 8, 128)),
+        held(given)
+        + [memory(DEVICES, 16, 128), memory(DEVICES, 8, 128), memory(2, NZ * CX, 128), memory(NZ * CX, CY)]
         + [memory(3, NZ, CX, CY), memory(2, 3, CX, 128), memory(2, 3, NZ, HALO, CY), memory(2, 3, ROWS, 128)]
         + [memory(1, NZ, CX, CY), memory(2, 1, CX, 128), memory(2, 1, NZ, HALO, CY), memory(2, 1, ROWS, 128)]
         + wide
-        + [dma((3,)), dma((GROUPS,)), dma((8,)), dma((8,)), dma((8,)), dma((8,))],
+        + [dma((6,)), dma((3,)), dma((GROUPS,)), dma((8,)), dma((8,)), dma((8,)), dma((8,))],
         dict(collective_id=0, has_side_effects=True),
-        count=6,
-    )(messages, pressure, conductivity, porosity, freeze_state, land_mask)
-    returned = call(
-        unroute_kernel, shaped(NZ, COLUMNS), [pltpu.VMEM((16, COLUMNS + 256), F32)], ins=[SMEM, VMEM]
-    )(ends, answer)
+        ins=[anywhere] * 6,
+    )(*given)
+    new_pressure, returned = call(
+        unroute_kernel,
+        (shaped(NZ, CX, CY), shaped(NZ, COLUMNS)),
+        [memory(8, COLUMNS + 256), memory(8, COLUMNS + 256), memory(DEVICES * 8, 128)],
+        ins=[SMEM, VMEM, VMEM],
+    )(ends, answer.reshape(DEVICES * 8, 128), pressure_now)
     return new_pressure, returned
 
 

time: 83.2 us -> 70.7 us (0.85)
  Pallas kernels: 81.6 us -> 69.9 us
    pallas_call x3, Pallas kernels: 81.6 us -> 69.9 us  [the longest x1 60.5 us: on_device(): call(interval_kernel, (shaped(NZ, CX, CY), shaped(DEVICES, 8, 128)), held...]
where the time goes in v2:
time: 70.7 us; the launch traced here: 70.6 us
  Pallas kernels  69.9 us (99%)
    pallas_call x1, Pallas kernels, on_device(): call(interval_kernel, (shaped(NZ, CX, CY), shaped(DEVICES, 8, 128)), held...  60.5 us
    pallas_call x1, Pallas kernels, on_device(): call(prep_kernel, (shaped(DEVICES, 16, 128), jax.ShapeDtypeStruct((8, 128...  5.72 us
    pallas_call x1, Pallas kernels, on_device(): call(unroute_kernel, (shaped(NZ, CX, CY), shaped(NZ, COLUMNS)), [memory(8...  3.69 us

profile of v2, /device:TPU:1, one launch (start us, length us, event | category | flops | bytes accessed | tf_op | source)
XLA Modules:
  0.0 70.6 jit_solution(152346301992326532)
XLA Ops:
  0.6 5.7 %shard_map.122 = (f32[128,16,128]{2,1,0:T(8,128)}, s32[8,128]{1,0:T(8,128)}) custom-call(s32[1,8192]{1,0:T(1,128)} %bitcast.6, s32[1,8192]{1,0:T(1,128)} %bitcast.7, f32[1,8192]{1,0:T(1,128)} %bitcast.8, f32[1,8192]{1,0:T(1,128)} %bitcast.9, f32[10,8192]{1,0:T(8,128)} %refs_4_.2, f32[10,8192]{1,0:T(8,128)} %refs_5_.2), custom_call_target="tpu_custom_call" | custom-call | tf_op jit(solution)/shard_map/pallas_call | solution.py:642
  6.4 60.5 %shard_map.123 = (f32[10,32,256]{2,1,0:T(8,128)}, f32[128,8,128]{2,1,0:T(8,128)}) custom-call(f32[128,16,128]{2,1,0:T(8,128)} %get-tuple-element.7.refs_0_, f32[10,32,256]{2,1,0:T(8,128)} %refs_1_.1, f32[10,32,256]{2,1,0:T(8,128)} %refs_2_.1, f32[10,32,256]{2,1,0:T(8,128)} %refs_3_.1, s32[10,32,256]{2,1,0:T(8,128)} %refs_4_.3, s32[32,256]{1,0:T(8,128)} %refs_5_.3), custom_call_target="tpu_custom_call" | custom-call | tf_op jit(solution)/shard_map/pallas_call | solution.py:650
  66.9 3.7 %shard_map.124 = (f32[10,32,256]{2,1,0:T(8,128)}, f32[10,8192]{1,0:T(8,128)}) custom-call(s32[8,128]{1,0:T(8,128)} %get-tuple-element.6.ends, f32[1024,128]{1,0:T(8,128)} %bitcast.5, f32[10,32,256]{2,1,0:T(8,128)} %get-tuple-element.9.pressure_ref), custom_call_target="tpu_custom_call" | custom-call | tf_op jit(solution)/shard_map/pallas_call | solution.py:662

commit v3 on v2

--- a/solution.py
+++ b/solution.py
@@ -399,7 +399,7 @@
         perm[k] = jnp.where(outside, 0.0, perm[k])
         return carry
 
-    lax.fori_loop(0, NZ, prepare, 0)
+    lax.fori_loop(0, NZ, prepare, 0, unroll=10)
 
     def faces(k, carry):
         here = perm[k]
@@ -408,7 +408,7 @@
         stored[k] = dry_inverse(p[k])[1]
         return carry
 
-    lax.fori_loop(0, NZ, faces, 0)
+    lax.fori_loop(0, NZ, faces, 0, unroll=10)
 
     def vertical_faces(k, carry):
         hz[k] = joined(perm[k], perm[k + 1])
@@ -423,7 +423,7 @@
         kr[k] = inverse * inverse * inverse
         return carry
 
-    lax.fori_loop(0, NZ, relative, 0)
+    lax.fori_loop(0, NZ, relative, 0, unroll=10)
 
     def layer(k, flow_above, last):
         here, rel = p[k], kr[k]
@@ -449,7 +449,7 @@
         scale[k] = OMEGA / jnp.where(diagonal > 0.0, diagonal, 1.0)
         return flow
 
-    flow = lax.fori_loop(0, NZ - 1, lambda k, f: layer(k, f, False), jnp.zeros((ROWS, LANES), F32))
+    flow = lax.fori_loop(0, NZ - 1, lambda k, f: layer(k, f, False), jnp.zeros((ROWS, LANES), F32), unroll=9)
     layer(NZ - 1, flow, True)
 
 
@@ -460,7 +460,7 @@
         u[k + 1] = opening
         return carry
 
-    lax.fori_loop(0, NZ, first, 0)
+    lax.fori_loop(0, NZ, first, 0, unroll=10)
     for old, new in ((u, v), (v, u), (u, v)):
 
         def sweep(k, carry, old=old, new=new):
@@ -471,13 +471,13 @@
             new[k + 1] = (1.0 - OMEGA) * here + start[k] + scale[k] * coupled
             return carry
 
-        lax.fori_loop(0, NZ, sweep, 0)
+        lax.fori_loop(0, NZ, sweep, 0, unroll=10)
 
     def advance(k, carry):
         p[k] = p[k] + v[k + 1]
         return carry
 
-    lax.fori_loop(0, NZ, advance, 0)
+    lax.fori_loop(0, NZ, advance, 0, unroll=10)
 
 
 def finish(p, pressure_out, saturated):

time: 70.7 us -> 65.2 us (0.922)
  Pallas kernels: 69.9 us -> 64.4 us
    pallas_call x1, Pallas kernels: 60.5 us -> 55 us  [on_device(): call(interval_kernel, (shaped(NZ, CX, CY), shaped(DEVICES, 8, 128)), held...]
where the time goes in v3:
time: 65.2 us; the launch traced here: 65 us
  Pallas kernels  64.4 us (99%)
    pallas_call x1, Pallas kernels, on_device(): call(interval_kernel, (shaped(NZ, CX, CY), shaped(DEVICES, 8, 128)), held...  55 us
    pallas_call x1, Pallas kernels, on_device(): call(prep_kernel, (shaped(DEVICES, 16, 128), jax.ShapeDtypeStruct((8, 128...  5.72 us
    pallas_call x1, Pallas kernels, on_device(): call(unroute_kernel, (shaped(NZ, CX, CY), shaped(NZ, COLUMNS)), [memory(8...  3.69 us

profile of v3, /device:TPU:1, one launch (start us, length us, event | category | flops | bytes accessed | tf_op | source)
XLA Modules:
  0.0 65.0 jit_solution(18054471128038609036)
XLA Ops:
  0.6 5.7 %shard_map.122 = (f32[128,16,128]{2,1,0:T(8,128)}, s32[8,128]{1,0:T(8,128)}) custom-call(s32[1,8192]{1,0:T(1,128)} %bitcast.6, s32[1,8192]{1,0:T(1,128)} %bitcast.7, f32[1,8192]{1,0:T(1,128)} %bitcast.8, f32[1,8192]{1,0:T(1,128)} %bitcast.9, f32[10,8192]{1,0:T(8,128)} %refs_4_.2, f32[10,8192]{1,0:T(8,128)} %refs_5_.2), custom_call_target="tpu_custom_call" | custom-call | tf_op jit(solution)/shard_map/pallas_call | solution.py:642
  6.4 55.0 %shard_map.123 = (f32[10,32,256]{2,1,0:T(8,128)}, f32[128,8,128]{2,1,0:T(8,128)}) custom-call(f32[128,16,128]{2,1,0:T(8,128)} %get-tuple-element.7.refs_0_, f32[10,32,256]{2,1,0:T(8,128)} %refs_1_.1, f32[10,32,256]{2,1,0:T(8,128)} %refs_2_.1, f32[10,32,256]{2,1,0:T(8,128)} %refs_3_.1, s32[10,32,256]{2,1,0:T(8,128)} %refs_4_.3, s32[32,256]{1,0:T(8,128)} %refs_5_.3), custom_call_target="tpu_custom_call" | custom-call | tf_op jit(solution)/shard_map/pallas_call | solution.py:650
  61.3 3.7 %shard_map.124 = (f32[10,32,256]{2,1,0:T(8,128)}, f32[10,8192]{1,0:T(8,128)}) custom-call(s32[8,128]{1,0:T(8,128)} %get-tuple-element.6.ends, f32[1024,128]{1,0:T(8,128)} %bitcast.5, f32[10,32,256]{2,1,0:T(8,128)} %get-tuple-element.9.pressure_ref), custom_call_target="tpu_custom_call" | custom-call | tf_op jit(solution)/shard_map/pallas_call | solution.py:662

commit v4 on v3

--- a/solution.py
+++ b/solution.py
@@ -217,7 +217,7 @@
     pltpu.make_async_copy(part, part, sem).wait()
 
 
-def send_replies(reply, answer, first, last, send_sem, recv_sem):
+def send_replies(reply, answer, first, count, send_sem, recv_sem):
     gx, gy = position()
     me = gx * GY + gy
 
@@ -232,7 +232,8 @@
         ).start()
         return carry
 
-    lax.fori_loop(first, last, send, 0)
+    for k in range(count):
+        send(first + k, 0)
 
 
 SIDES = tuple((dx, dy) for dx in (-1, 0, 1) for dy in (-1, 0, 1) if (dx, dy) != (0, 0))
@@ -490,12 +491,15 @@
         saturated[1, rows, :] = sat[:, 128:256]
 
 
-def gather_group(saturated, incoming, group, reply):
+def split_lines(saturated):
+    every = jnp.concatenate([saturated[0], saturated[1]], axis=1)
+    high = every.astype(BF16)
+    return jnp.concatenate([high, (every - high.astype(F32)).astype(BF16)], axis=1)
+
+
+def gather_group(left, incoming, group, reply):
     lane = iota((8, 128), 1)
     row = iota((8, 128), 0)
-    every = jnp.concatenate([saturated[0], saturated[1]], axis=1)
-    high = every.astype(BF16)
-    left = jnp.concatenate([high, (every - high.astype(F32)).astype(BF16)], axis=1)
     for pair in range(GROUP // 8):
         at = group * (GROUP // 4) + 2 * pair
         tiles = compact(incoming, at) + compact(incoming, at + 1)
@@ -592,17 +596,20 @@
     linearize(perm, porosity, p, stored, kr, hx, hy, hz, gx_, gy_, gz, scale, start)
     smooth(p, src, gx_, gy_, gz, scale, start, u, v)
     finish(p, pressure_out, saturated)
-    gather_group(saturated, incoming, 0, reply)
-    send_replies(reply, answer, 1, GROUP, sems.at[1], sems.at[2])
+    left = split_lines(saturated)
+    gather_group(left, incoming, 0, reply)
+    send_replies(reply, answer, 1, GROUP - 1, sems.at[1], sems.at[2])
+    gather_group(left, incoming, 1, reply)
     gx, gy = position()
     answer[gx * GY + gy] = reply[0]
 
     def depart(group, carry):
-        gather_group(saturated, incoming, group, reply)
-        send_replies(reply, answer, group * GROUP, group * GROUP + GROUP, sems.at[1], sems.at[2])
-        return carry
-
-    lax.fori_loop(1, GROUPS, depart, 0)
+        send_replies(reply, answer, (group - 1) * GROUP, GROUP, sems.at[1], sems.at[2])
+        gather_group(left, incoming, group, reply)
+        return carry
+
+    lax.fori_loop(2, GROUPS, depart, 0)
+    send_replies(reply, answer, DEVICES - GROUP, GROUP, sems.at[1], sems.at[2])
     for copy in halos + copies:
         copy.wait_send()
     wait_for(messages, 1, DEVICES - 1, SENT, sems.at[0])

time: 65.2 us -> 63.9 us (0.980)
  Pallas kernels: 64.4 us -> 63.1 us
    pallas_call x1, Pallas kernels: 55 us -> 53.7 us  [on_device(): call(interval_kernel, (shaped(NZ, CX, CY), shaped(DEVICES, 8, 128)), held...]
where the time goes in v4:
time: 63.9 us; the launch traced here: 63.8 us
  Pallas kernels  63.1 us (99%)
  between operations  0.65 us (1%)
    pallas_call x1, Pallas kernels, on_device(): call(interval_kernel, (shaped(NZ, CX, CY), shaped(DEVICES, 8, 128)), held...  53.7 us
    pallas_call x1, Pallas kernels, on_device(): call(prep_kernel, (shaped(DEVICES, 16, 128), jax.ShapeDtypeStruct((8, 128...  5.72 us
    pallas_call x1, Pallas kernels, on_device(): call(unroute_kernel, (shaped(NZ, CX, CY), shaped(NZ, COLUMNS)), [memory(8...  3.69 us

profile of v4, /device:TPU:1, one launch (start us, length us, event | category | flops | bytes accessed | tf_op | source)
XLA Modules:
  0.0 63.8 jit_solution(7790001448107674561)
XLA Ops:
  0.6 5.7 %shard_map.122 = (f32[128,16,128]{2,1,0:T(8,128)}, s32[8,128]{1,0:T(8,128)}) custom-call(s32[1,8192]{1,0:T(1,128)} %bitcast.6, s32[1,8192]{1,0:T(1,128)} %bitcast.7, f32[1,8192]{1,0:T(1,128)} %bitcast.8, f32[1,8192]{1,0:T(1,128)} %bitcast.9, f32[10,8192]{1,0:T(8,128)} %refs_4_.2, f32[10,8192]{1,0:T(8,128)} %refs_5_.2), custom_call_target="tpu_custom_call" | custom-call | tf_op jit(solution)/shard_map/pallas_call | solution.py:649
  6.4 53.7 %shard_map.123 = (f32[10,32,256]{2,1,0:T(8,128)}, f32[128,8,128]{2,1,0:T(8,128)}) custom-call(f32[128,16,128]{2,1,0:T(8,128)} %get-tuple-element.7.refs_0_, f32[10,32,256]{2,1,0:T(8,128)} %refs_1_.1, f32[10,32,256]{2,1,0:T(8,128)} %refs_2_.1, f32[10,32,256]{2,1,0:T(8,128)} %refs_3_.1, s32[10,32,256]{2,1,0:T(8,128)} %refs_4_.3, s32[32,256]{1,0:T(8,128)} %refs_5_.3), custom_call_target="tpu_custom_call" | custom-call | tf_op jit(solution)/shard_map/pallas_call | solution.py:657
  60.1 3.7 %shard_map.124 = (f32[10,32,256]{2,1,0:T(8,128)}, f32[10,8192]{1,0:T(8,128)}) custom-call(s32[8,128]{1,0:T(8,128)} %get-tuple-element.6.ends, f32[1024,128]{1,0:T(8,128)} %bitcast.5, f32[10,32,256]{2,1,0:T(8,128)} %get-tuple-element.9.pressure_ref), custom_call_target="tpu_custom_call" | custom-call | tf_op jit(solution)/shard_map/pallas_call | solution.py:669

commit v5 on v4

--- a/solution.py
+++ b/solution.py
@@ -177,8 +177,12 @@
 
 def device_at(offset):
     gx, gy = position()
-    flat = lax.rem(gx * GY + gy + offset, DEVICES)
-    return flat // GY, lax.rem(flat, GY)
+    return lax.rem(gx + offset // GY, GX), lax.rem(gy + lax.rem(offset, GY), GY)
+
+
+def device_before(offset):
+    gx, gy = position()
+    return lax.rem(gx - offset // GY + GX, GX), lax.rem(gy - lax.rem(offset, GY) + GY, GY)
 
 
 def neighbour(dx, dy):
@@ -227,7 +231,7 @@
             dst_ref=answer.at[me, pl.ds(0, 8)],
             send_sem=send_sem,
             recv_sem=recv_sem,
-            device_id=device_at(DEVICES - k),
+            device_id=device_before(k),
             device_id_type=MESH,
         ).start()
         return carry

time: 63.9 us -> 62.9 us (0.984)
  Pallas kernels: 63.1 us -> 62.1 us
    pallas_call x1, Pallas kernels: 53.7 us -> 52.7 us  [on_device(): call(interval_kernel, (shaped(NZ, CX, CY), shaped(DEVICES, 8, 128)), held...]
where the time goes in v5:
time: 62.9 us; the launch traced here: 62.8 us
  Pallas kernels  62.1 us (99%)
  between operations  0.65 us (1%)
    pallas_call x1, Pallas kernels, on_device(): call(interval_kernel, (shaped(NZ, CX, CY), shaped(DEVICES, 8, 128)), held...  52.7 us
    pallas_call x1, Pallas kernels, on_device(): call(prep_kernel, (shaped(DEVICES, 16, 128), jax.ShapeDtypeStruct((8, 128...  5.72 us
    pallas_call x1, Pallas kernels, on_device(): call(unroute_kernel, (shaped(NZ, CX, CY), shaped(NZ, COLUMNS)), [memory(8...  3.69 us

profile of v5, /device:TPU:1, one launch (start us, length us, event | category | flops | bytes accessed | tf_op | source)
XLA Modules:
  0.0 62.8 jit_solution(10680046501832885607)
XLA Ops:
  0.6 5.7 %shard_map.122 = (f32[128,16,128]{2,1,0:T(8,128)}, s32[8,128]{1,0:T(8,128)}) custom-call(s32[1,8192]{1,0:T(1,128)} %bitcast.6, s32[1,8192]{1,0:T(1,128)} %bitcast.7, f32[1,8192]{1,0:T(1,128)} %bitcast.8, f32[1,8192]{1,0:T(1,128)} %bitcast.9, f32[10,8192]{1,0:T(8,128)} %refs_4_.2, f32[10,8192]{1,0:T(8,128)} %refs_5_.2), custom_call_target="tpu_custom_call" | custom-call | tf_op jit(solution)/shard_map/pallas_call | solution.py:653
  6.4 52.7 %shard_map.123 = (f32[10,32,256]{2,1,0:T(8,128)}, f32[128,8,128]{2,1,0:T(8,128)}) custom-call(f32[128,16,128]{2,1,0:T(8,128)} %get-tuple-element.7.refs_0_, f32[10,32,256]{2,1,0:T(8,128)} %refs_1_.1, f32[10,32,256]{2,1,0:T(8,128)} %refs_2_.1, f32[10,32,256]{2,1,0:T(8,128)} %refs_3_.1, s32[10,32,256]{2,1,0:T(8,128)} %refs_4_.3, s32[32,256]{1,0:T(8,128)} %refs_5_.3), custom_call_target="tpu_custom_call" | custom-call | tf_op jit(solution)/shard_map/pallas_call | solution.py:661
  59.1 3.7 %shard_map.124 = (f32[10,32,256]{2,1,0:T(8,128)}, f32[10,8192]{1,0:T(8,128)}) custom-call(s32[8,128]{1,0:T(8,128)} %get-tuple-element.6.ends, f32[1024,128]{1,0:T(8,128)} %bitcast.5, f32[10,32,256]{2,1,0:T(8,128)} %get-tuple-element.9.pressure_ref), custom_call_target="tpu_custom_call" | custom-call | tf_op jit(solution)/shard_map/pallas_call | solution.py:673
